TPU v7x, 32 devices: a whole 2x2x4 slice. The times are simulated.
32 devices in a mesh: groups: 2 (over y), row: 4 (over z), col: 4 (over x, core), rep: 1.
Axes of the slice: x: 2, y: 2, z: 4, core: 2. Of those that a mesh axis runs over, the one named last changes fastest.
Arguments:
- sequences: int32 [256, 160], P(('groups', 'rep')), parts along dimension 0, may hold values from 0 to 20
- seq_weights: float32 [256], P('groups'), parts along dimension 0, may hold values from 0.2 to 1
- fields: float32 [320, 21], P(('groups', 'row', 'col')), parts along dimension 0, may hold values from -3 to 3
- couplings: float32 [6720, 4, 4, 210], P(('groups', 'row', 'rep'), 'col'), parts along dimension 0, may hold values from -0.18 to 0.18
Outputs:
- new_couplings: float32 [6720, 4, 4, 210], P(('groups', 'row', 'rep'), 'col'), parts along dimension 0
- new_fields: float32 [320, 21], P(('groups', 'row', 'col')), parts along dimension 0
There are 2 independent parts, one for each index of `groups`. A program takes and returns all parts, laid end to end along the dimension named above; each array names one. Nothing has to cross between parts.
All inputs are finite; a program needn't handle non-finite values.
Results may differ from a plain program's by a relative error of at most 0.0029.
Values may be sent and summed in bfloat16 or wider, within the bound.
A program may use at most 128 MiB of HBM per device.

v0:
```python
import jax
import jax.numpy as jnp
from jax import lax
from jax.sharding import PartitionSpec as P

STEPS = 2


learn_rate = 2.0
shrink = 0.02


def per_device(sequences, seq_weights, fields, couplings):
    half_rows = couplings.shape[0]
    row_count = couplings.shape[2]
    block_width = couplings.shape[3]
    own_sites = fields.shape[0]
    states = fields.shape[1]
    seq_count = sequences.shape[0]
    col_count = lax.axis_size("col")
    row_index = lax.axis_index("row")
    col_index = lax.axis_index("col")
    rep_index = lax.axis_index("rep")
    row_sites = own_sites * col_count
    row_width = row_sites * states
    global_rows = (
        row_index * row_width + rep_index * half_rows + jnp.arange(half_rows, dtype=jnp.int32)
    )
    row_site = global_rows // states
    block_pos = jnp.arange(row_count, dtype=jnp.int32)[:, None]
    within = jnp.arange(block_width, dtype=jnp.int32)[None, :] // states
    col_site = (block_pos * col_count + col_index) * own_sites + within
    off_diagonal = (row_site[:, None, None, None] != col_site[None, None, :, :]).astype(jnp.float32)
    coupl = couplings * off_diagonal
    weight_total = jnp.sum(seq_weights)
    own_weights = lax.dynamic_slice_in_dim(seq_weights, rep_index * seq_count, seq_count)
    seq_row = lax.dynamic_slice_in_dim(sequences, row_index * row_sites, row_sites, 1)
    seq_col = lax.dynamic_index_in_dim(
        sequences.reshape(seq_count, row_count, col_count, own_sites), col_index, 2, keepdims=False
    )
    seq_col = seq_col.reshape(seq_count, row_count * own_sites)
    seq_mine = lax.dynamic_slice_in_dim(seq_row, col_index * own_sites, own_sites, 1)
    levels = jnp.arange(states, dtype=jnp.int32)

    def encode(codes):
        return (
            (codes[:, :, None] == levels[None, None, :])
            .astype(jnp.bfloat16)
            .reshape(codes.shape[0], codes.shape[1] * states)
        )

    onehot_row = encode(seq_row)
    onehot_col = encode(seq_col)
    mine_onehot = (seq_mine.T[:, None, :] == levels[None, :, None]).astype(jnp.float32)
    every_row, every_col = (
        lax.all_gather(seq_row, "rep", axis=0, tiled=True),
        lax.all_gather(seq_col, "rep", axis=0, tiled=True),
    )
    wide_row = lax.dynamic_slice_in_dim(encode(every_row), rep_index * half_rows, half_rows, 1)
    wide_col = encode(every_col)
    for iteration in range(STEPS):
        narrow_rows = coupl.reshape(half_rows, row_count * block_width).astype(jnp.bfloat16)
        gathered = lax.all_gather(narrow_rows, "rep", axis=0, tiled=True)
        direct = lax.psum_scatter(
            lax.dot_general(
                gathered, onehot_row, (((0,), (1,)), ((), ())), preferred_element_type=jnp.float32
            ).astype(jnp.bfloat16),
            "row",
            scatter_dimension=0,
            tiled=True,
        ).astype(jnp.float32)
        transposed = lax.psum_scatter(
            lax.dot_general(
                gathered, onehot_col, (((1,), (1,)), ((), ())), preferred_element_type=jnp.float32
            ).astype(jnp.bfloat16),
            "col",
            scatter_dimension=0,
            tiled=True,
        ).astype(jnp.float32)
        logits = (direct + transposed).reshape(own_sites, states, seq_count) + fields[:, :, None]
        powers = jnp.exp(logits)
        probability = powers / jnp.sum(powers, axis=1, keepdims=True)
        resid = (own_weights[None, None, :] * (probability - mine_onehot)).astype(jnp.bfloat16)
        resid = resid.reshape(block_width, seq_count)
        all_resid = lax.all_gather(resid, "rep", axis=1, tiled=True)
        field_grad = jnp.sum(all_resid, axis=1, dtype=jnp.float32)
        by_row = lax.all_gather(all_resid, "row", axis=0, tiled=True)
        by_col = lax.all_gather(all_resid, "col", axis=0, tiled=True)
        mine_rows = lax.dynamic_slice_in_dim(by_col, rep_index * half_rows, half_rows, 0)
        first = lax.dot_general(
            wide_row, by_row, (((0,), (1,)), ((), ())), preferred_element_type=jnp.float32
        )
        second = lax.dot_general(
            mine_rows, wide_col, (((1,), (0,)), ((), ())), preferred_element_type=jnp.float32
        )
        coupling_grad = first + second
        coupling_grad = coupling_grad.reshape(half_rows, 1, row_count, block_width)
        coupl = coupl - learn_rate * (off_diagonal * coupling_grad / weight_total + shrink * coupl)
        fields = fields - learn_rate * (
            field_grad.reshape(own_sites, states) / weight_total + shrink * fields
        )
    return (coupl, fields)


def solution(mesh):
    in_specs = (
        P(("groups", "rep"), None),
        P("groups"),
        P(("groups", "row", "col"), None),
        P(("groups", "row", "rep"), "col", None, None),
    )
    out_specs = (P(("groups", "row", "rep"), "col", None, None), P(("groups", "row", "col"), None))
    return jax.shard_map(
        per_device, mesh=mesh, in_specs=in_specs, out_specs=out_specs, check_vma=False
    )
```

profile of v0, /device:TPU:0, one launch (start us, length us, event | category | flops | bytes accessed | tf_op | source)
XLA Modules:
  0.0 156.9 jit_solution(12268254585393619638)
XLA Ops:
  0.7 0.7 constant_dynamic-slice_fusion.1
  1.4 0.1 iota_compare_fusion.1
  1.5 0.1 eq.121
  1.6 0.1 broadcast_add_fusion
  1.7 2.2 %fusion.14 = bf16[840,1,4,210]{0,3,2,1:T(8,128)(2,1)S(1)} fusion(f32[840,1,4,210]{0,2,3,1:T(4,128)} %param.7, s32[4,210]{1,0:T(4,128)S(1)} %broadcast_add_fusion, s32[840]{0:T(1024)S(1)} %add_select_fusion), kind=kLoop, calls=%fused_computation.13 | loop fusion | flops 1411200 | bytes 4240320 | tf_op jit(solution)/shard_map/convert_element_type | solution.py:62
  3.9 0.7 convert_element_type.63
  4.6 0.6 convolution_convert_fusion.3
  5.2 16.0 %fusion = bf16[224,128]{1,0:T(8,128)(2,1)S(1)} fusion(bf16[840,128]{1,0:T(8,128)(2,1)S(1)} %convolution_convert_fusion.3), kind=kCustom, calls=%all-reduce-scatter | all-reduce-scatter fusion | flops 114689 | bytes 272896
  21.3 2.4 %collective-permute-start = (bf16[42,128]{1,0:T(8,128)(2,1)S(1)}, bf16[42,128]{1,0:T(8,128)(2,1)S(1)}, u32[]{:S(2)}, u32[]{:S(2)}) collective-permute-start(bf16[42,128]{1,0:T(8,128)(2,1)S(1)} %slice), channel_id=1, source_target_pairs={{0,4},{4,8},{8,12},{1,5},{5,9},{9,13},{2,6},{6,10},{10,14},{3,7},{... | collective-permute-start | bytes 32264
  23.7 0.1 iota_compare_fusion
  23.8 0.1 eq.126
  23.9 0.0 copy-start.15
  23.9 0.0 copy-start.14
  23.9 0.7 convolution_convert_fusion.2
  24.6 8.8 %fusion.1 = bf16[224,128]{1,0:T(8,128)(2,1)S(1)} fusion(bf16[840,128]{1,0:T(8,128)(2,1)S(1)} %convolution_convert_fusion.2), kind=kCustom, calls=%all-reduce-scatter.1 | all-reduce-scatter fusion | flops 114689 | bytes 272896
  33.4 1.3 collective-permute-start.1
  34.8 0.1 eq.116
  35.0 0.2 broadcast_compare_fusion
  35.3 0.6 dynamic-slice.14
  35.9 0.6 dynamic-slice.10
  37.8 0.1 add.142
  37.8 0.1 eq.130
  38.0 0.7 reduce_sum.46
  38.7 0.4 concatenate
  39.1 0.4 concatenate.1
  39.5 0.9 fusion.5
  40.5 1.3 convert_reduce_fusion.1
  41.8 6.0 %all-gather.1 = bf16[4,210,128]{2,1,0:T(8,128)(2,1)S(1)} all-gather(bf16[1,210,128]{2,1,0:T(8,128)(2,1)S(1)} %bitcast.50), channel_id=1, replica_groups=mesh['groups'=2,'row'=4,'col'=4,'rep'=1] {'col'}, dimensions={0}, use_global_device_ids=true | all-gather | bytes 268800 | tf_op jit(solution)/shard_map/all_gather | solution.py:88
  47.7 14.1 %all-gather = bf16[4,210,128]{2,1,0:T(8,128)(2,1)S(1)} all-gather(bf16[1,210,128]{2,1,0:T(8,128)(2,1)S(1)} %bitcast.51), channel_id=1, replica_groups=mesh['groups'=2,'row'=4,'col'=4,'rep'=1] {'row'}, dimensions={0}, use_global_device_ids=true | all-gather | bytes 268800 | tf_op jit(solution)/shard_map/all_gather | solution.py:87
  61.9 0.1 reshape.296
  62.0 0.1 reshape.294
  62.0 0.6 fusion.29
  62.7 2.3 %convolution_add_fusion.1 = f32[840,840]{0,1:T(8,128)} fusion(f32[840,840]{0,1:T(8,128)S(1)} %fusion.29, bf16[840,128]{1,0:T(8,128)(2,1)S(1)} %reshape.296, pred[128,840]{0,1:T(8,128)(4,1)S(1)} %get-tuple-element.11), kind=kOutput, calls=%fused_computation.15 | convolution fusion | flops 181339200 | bytes 5967360 | tf_op jit(solution)/shard_map/dot_general | solution.py:93
  64.9 2.2 %reshape.290 = f32[840,1,4,210]{0,3,2,1:T(8,128)S(1)} reshape(f32[840,840]{0,1:T(8,128)} %convolution_add_fusion.1) | data formatting | bytes 5644800 | tf_op jit(solution)/shard_map/reshape | solution.py:97
  67.2 4.6 %fusion.26 = bf16[840,1,4,210]{0,3,2,1:T(8,128)(2,1)} fusion(f32[]{:T(128)} %reduce_sum.46, f32[840,1,4,210]{0,3,2,1:T(8,128)S(1)} %reshape.290, f32[840,1,4,210]{0,2,3,1:T(4,128)} %param.7, s32[4,210]{1,0:T(4,128)S(1)} %broadcast_add_fusion, s32[840]{0:T(1024)S(1)} %add_select_fusion), kind=kLoop, calls=%fused_computation.61 | loop fusion | flops 6350400 | bytes 7062724 | tf_op jit(solution)/shard_map/convert_element_type | solution.py:62
  71.8 3.3 %convert_element_type.71 = bf16[840,840]{0,1:T(8,128)(2,1)} reshape(bf16[840,1,4,210]{0,3,2,1:T(8,128)(2,1)} %fusion.26) | data formatting | bytes 2822400 | tf_op jit(solution)/shard_map/convert_element_type | solution.py:62
  75.1 2.7 %convolution_convert_fusion = bf16[840,128]{1,0:T(8,128)(2,1)} fusion(bf16[840,840]{0,1:T(8,128)(2,1)} %convert_element_type.71, pred[128,840]{0,1:T(8,128)(4,1)S(1)} %copy-done.6), kind=kOutput, calls=%fused_computation.16 | convolution fusion | flops 180741120 | bytes 1733760 | tf_op jit(solution)/shard_map/dot_general | solution.py:73
  77.8 2.7 %convolution_convert_fusion.1 = bf16[840,128]{1,0:T(8,128)(2,1)} fusion(bf16[840,840]{0,1:T(8,128)(2,1)} %convert_element_type.71, pred[128,840]{0,1:T(8,128)(4,1)S(1)} %copy-done.4), kind=kOutput, calls=%fused_computation.17 | convolution fusion | flops 180741120 | bytes 1733760 | tf_op jit(solution)/shard_map/dot_general | solution.py:65
  80.5 0.7 broadcast_divide_fusion.1
  81.2 0.1 div.94
  81.3 13.7 %fusion.2 = bf16[224,128]{1,0:T(8,128)(2,1)S(1)} fusion(bf16[840,128]{1,0:T(8,128)(2,1)} %convolution_convert_fusion.1), kind=kCustom, calls=%all-reduce-scatter.2 | all-reduce-scatter fusion | flops 114689 | bytes 272896
  95.0 8.7 %fusion.3 = bf16[224,128]{1,0:T(8,128)(2,1)S(1)} fusion(bf16[840,128]{1,0:T(8,128)(2,1)} %convolution_convert_fusion), kind=kCustom, calls=%all-reduce-scatter.3 | all-reduce-scatter fusion | flops 114689 | bytes 272896
  103.7 1.3 collective-permute-start.2
  105.0 1.3 collective-permute-start.3
  106.3 0.7 add.152
  107.0 0.4 concatenate.2
  107.4 2.0 %concatenate.3 = bf16[266,128]{1,0:T(8,128)(2,1)} concatenate(bf16[42,128]{1,0:T(8,128)(2,1)S(1)} %collective-permute-done.3, bf16[224,128]{1,0:T(8,128)(2,1)S(1)} %fusion.3), dimensions={0} | concatenate | bytes 136192
  109.4 0.8 convert_add_fusion
  110.2 0.7 reshape.291
  110.9 1.0 fusion.4
  111.9 0.7 div.96
  112.5 1.1 convert_reduce_fusion
  113.6 8.3 %all-gather.3 = bf16[4,210,128]{2,1,0:T(8,128)(2,1)} all-gather(bf16[1,210,128]{2,1,0:T(8,128)(2,1)S(1)} %bitcast.52), channel_id=1, replica_groups=mesh['groups'=2,'row'=4,'col'=4,'rep'=1] {'col'}, dimensions={0}, use_global_device_ids=true | all-gather | bytes 268800 | tf_op jit(solution)/shard_map/all_gather | solution.py:88
  121.9 15.1 %all-gather.2 = bf16[4,210,128]{2,1,0:T(8,128)(2,1)} all-gather(bf16[1,210,128]{2,1,0:T(8,128)(2,1)S(1)} %bitcast.53), channel_id=1, replica_groups=mesh['groups'=2,'row'=4,'col'=4,'rep'=1] {'row'}, dimensions={0}, use_global_device_ids=true | all-gather | bytes 268800 | tf_op jit(solution)/shard_map/all_gather | solution.py:87
  137.0 0.7 broadcast_divide_fusion
  137.7 0.1 div.100
  137.8 1.3 multiply_subtract_fusion
  139.1 1.7 %reshape.300 = bf16[840,128]{1,0:T(8,128)(2,1)} reshape(bf16[4,210,128]{2,1,0:T(8,128)(2,1)} %all-gather.3) | data formatting | bytes 430080
  140.8 1.7 %reshape.298 = bf16[840,128]{1,0:T(8,128)(2,1)} reshape(bf16[4,210,128]{2,1,0:T(8,128)(2,1)} %all-gather.2) | data formatting | bytes 430080
  142.4 1.6 %fusion.30 = f32[840,840]{0,1:T(8,128)S(1)} fusion(pred[128,840]{0,1:T(8,128)(4,1)S(1)} %get-tuple-element.12, bf16[840,128]{1,0:T(8,128)(2,1)} %reshape.298), kind=kOutput, calls=%fused_computation.63 | convolution fusion | flops 180633600 | bytes 3144960 | tf_op jit(solution)/shard_map/dot_general | solution.py:90
  144.1 2.3 %convolution_add_fusion = f32[840,840]{0,1:T(8,128)} fusion(f32[840,840]{0,1:T(8,128)S(1)} %fusion.30, bf16[840,128]{1,0:T(8,128)(2,1)S(1)} %copy-done, pred[128,840]{0,1:T(8,128)(4,1)S(1)} %get-tuple-element.11), kind=kOutput, calls=%fused_computation.14 | convolution fusion | flops 181339200 | bytes 5967360 | tf_op jit(solution)/shard_map/dot_general | solution.py:93
  146.3 3.8 %reshape.292 = f32[840,1,4,210]{0,3,2,1:T(8,128)} reshape(f32[840,840]{0,1:T(8,128)} %convolution_add_fusion) | data formatting | bytes 5644800 | tf_op jit(solution)/shard_map/reshape | solution.py:97
  150.2 4.3 %fusion.13 = f32[840,1,4,210]{0,3,2,1:T(8,128)S(1)} fusion(f32[840,1,4,210]{0,3,2,1:T(8,128)} %reshape.292, f32[]{:T(128)} %reduce_sum.46, s32[4,210]{1,0:T(4,128)S(1)} %copy-done.11, s32[840]{0:T(1024)S(1)} %copy-done.9, f32[840,1,4,210]{0,3,2,1:T(8,128)S(1)} %reshape.290, f32[840,1,4,210]{0,2,3,1:T(4,128)} %param.7), kind=kLoop, calls=%fused_computation.12 | loop fusion | flops 9878400 | bytes 11296324 | tf_op jit(solution)/shard_map/sub | solution.py:98
  154.5 2.4 %copy.12 = f32[840,1,4,210]{0,2,3,1:T(4,128)} copy(f32[840,1,4,210]{0,3,2,1:T(8,128)S(1)} %fusion.13) | data formatting | bytes 5644800
  (57 shorter events, 0.4 us)
Async XLA Ops:
  0.7 66.4 %copy-start.8 = (s32[840]{0:T(1024)}, s32[840]{0:T(1024)S(1)}, u32[]{:S(2)}) copy-start(s32[840]{0:T(1024)S(1)} %add_select_fusion) | copy-start | bytes 10084
  1.6 3.0 %copy-start.3 = (pred[128,840]{0,1:T(8,128)(4,1)}, pred[128,840]{0,1:T(8,128)(4,1)S(1)}, u32[]{:S(2)}) copy-start(pred[128,840]{0,1:T(8,128)(4,1)S(1)} %eq.121) | copy-start | bytes 322564
  1.7 65.4 %copy-start.10 = (s32[4,210]{1,0:T(4,128)}, s32[4,210]{1,0:T(4,128)S(1)}, u32[]{:S(2)}) copy-start(s32[4,210]{1,0:T(4,128)S(1)} %broadcast_add_fusion) | copy-start | bytes 10084
  3.9 19.7 %copy-start.1 = (s32[128,160]{0,1:T(8,128)S(1)}, s32[128,160]{0,1:T(8,128)}, u32[]{:S(2)}) copy-start(s32[128,160]{0,1:T(8,128)} %param.4) | copy-start | bytes 245764
  21.3 17.4 %collective-permute-start = (bf16[42,128]{1,0:T(8,128)(2,1)S(1)}, bf16[42,128]{1,0:T(8,128)(2,1)S(1)}, u32[]{:S(2)}, u32[]{:S(2)}) collective-permute-start(bf16[42,128]{1,0:T(8,128)(2,1)S(1)} %slice), channel_id=1, source_target_pairs={{0,4},{4,8},{8,12},{1,5},{5,9},{9,13},{2,6},{6,10},{10,14},{3,7},{... | collective-permute-start | bytes 32264
  23.9 11.2 %copy-start.5 = (pred[128,840]{0,1:T(8,128)(4,1)}, pred[128,840]{0,1:T(8,128)(4,1)S(1)}, u32[]{:S(2)}) copy-start(pred[128,840]{0,1:T(8,128)(4,1)S(1)} %eq.126) | copy-start | bytes 322564
  23.9 11.4 %copy-start.15 = (u32[32]{0:T(128)S(1)}, u32[32]{0:T(128)}, u32[]{:S(2)}) copy-start(u32[32]{0:T(128)} %constant.72) | copy-start | bytes 388
  23.9 12.0 %copy-start.14 = (u32[32]{0:T(128)S(1)}, u32[32]{0:T(128)}, u32[]{:S(2)}) copy-start(u32[32]{0:T(128)} %constant.68) | copy-start | bytes 388
  23.9 13.9 %copy-start.7 = (f32[10,21]{1,0:T(8,128)S(1)}, f32[10,21]{1,0:T(8,128)}, u32[]{:S(2)}) copy-start(f32[10,21]{1,0:T(8,128)} %param.6) | copy-start | bytes 2524
  23.9 14.1 %copy-start.13 = (f32[128]{0:T(128)S(1)}, f32[128]{0:T(128)}, u32[]{:S(2)}) copy-start(f32[128]{0:T(128)} %param.5) | copy-start | bytes 1540
  33.4 5.6 %collective-permute-start.1 = (bf16[42,128]{1,0:T(8,128)(2,1)S(1)}, bf16[42,128]{1,0:T(8,128)(2,1)S(1)}, u32[]{:S(2)}, u32[]{:S(2)}) collective-permute-start(bf16[42,128]{1,0:T(8,128)(2,1)S(1)} %slice.1), channel_id=1, source_target_pairs={{0,1},{1,2},{2,3},{4,5},{5,6},{6,7},{8,9},{9,10},{10,11},{12,13},{... | collective-permute-start | bytes 32264
  67.1 7.9 %copy-start.6 = (pred[128,840]{0,1:T(8,128)(4,1)S(1)}, pred[128,840]{0,1:T(8,128)(4,1)}, u32[]{:S(2)}) copy-start(pred[128,840]{0,1:T(8,128)(4,1)} %copy-done.5) | copy-start | bytes 322564
  71.8 6.0 %copy-start.4 = (pred[128,840]{0,1:T(8,128)(4,1)S(1)}, pred[128,840]{0,1:T(8,128)(4,1)}, u32[]{:S(2)}) copy-start(pred[128,840]{0,1:T(8,128)(4,1)} %copy-done.3) | copy-start | bytes 322564
  71.8 8.7 %copy-start.12 = (f32[210]{0:T(256)S(1)}, f32[210]{0:T(256)}, u32[]{:S(2)}) copy-start(f32[210]{0:T(256)} %get-tuple-element.8) | copy-start | bytes 2524
  103.7 3.3 %collective-permute-start.2 = (bf16[42,128]{1,0:T(8,128)(2,1)S(1)}, bf16[42,128]{1,0:T(8,128)(2,1)S(1)}, u32[]{:S(2)}, u32[]{:S(2)}) collective-permute-start(bf16[42,128]{1,0:T(8,128)(2,1)S(1)} %slice.2), channel_id=1, source_target_pairs={{0,4},{4,8},{8,12},{1,5},{5,9},{9,13},{2,6},{6,10},{10,14},{3,7},{... | collective-permute-start | bytes 32264
  105.0 2.4 %collective-permute-start.3 = (bf16[42,128]{1,0:T(8,128)(2,1)S(1)}, bf16[42,128]{1,0:T(8,128)(2,1)S(1)}, u32[]{:S(2)}, u32[]{:S(2)}) collective-permute-start(bf16[42,128]{1,0:T(8,128)(2,1)S(1)} %slice.3), channel_id=1, source_target_pairs={{0,1},{1,2},{2,3},{4,5},{5,6},{6,7},{8,9},{9,10},{10,11},{12,13},{... | collective-permute-start | bytes 32264
  106.3 1.1 copy-start.2
  142.4 1.6 %copy-start = (bf16[840,128]{1,0:T(8,128)(2,1)S(1)}, bf16[840,128]{1,0:T(8,128)(2,1)}, u32[]{:S(2)}) copy-start(bf16[840,128]{1,0:T(8,128)(2,1)} %reshape.300) | copy-start | bytes 645124
  146.3 3.9 %copy-start.9 = (s32[840]{0:T(1024)S(1)}, s32[840]{0:T(1024)}, u32[]{:S(2)}) copy-start(s32[840]{0:T(1024)} %copy-done.8) | copy-start | bytes 10084
  146.3 3.9 %copy-start.11 = (s32[4,210]{1,0:T(4,128)S(1)}, s32[4,210]{1,0:T(4,128)}, u32[]{:S(2)}) copy-start(s32[4,210]{1,0:T(4,128)} %copy-done.10) | copy-start | bytes 10084
where the time goes:
time: 158 us; the launch traced here: 157 us
  blocking collectives  90.6 us (57%)
  local copies, waits for them, and re-layouts  23.9 us (15%)
  other arithmetic  20.2 us (13%)
  matrix products  13.5 us (9%)
  starting transfers between devices  6.23 us (4%)
  between operations  2.53 us (2%)
    unnamed x4, blocking collectives  47.1 us
    all_gather x2, blocking collectives, per_device(): by_row = lax.all_gather(all_resid, 'row', axis=0, tiled=True)  29.2 us
    all_gather x2, blocking collectives, per_device(): by_col = lax.all_gather(all_resid, 'col', axis=0, tiled=True)  14.2 us
    unnamed x47, local copies, waits for them, and re-layouts  10.3 us
    convert_element_type x2, other arithmetic, per_device(): coupl.reshape(half_rows, row_count * block_width).astype(jnp.bfloat16)  6.83 us
    unnamed x4, starting transfers between devices  6.23 us
    reshape x2, local copies, waits for them, and re-layouts, per_device(): coupling_grad = coupling_grad.reshape(half_rows, 1, row_count, block_width)  6.04 us
    dot_general x2, matrix products, per_device(): lax.dot_general(mine_rows, wide_col, (((1,), (0,)), ((), ())), preferred_...  4.51 us
  transfers between devices with their start and end apart: 4, of which 0 were waited for; matrix products, arithmetic and copies ran while one was open for 9% of the time, Pallas kernels for 0%

commit v1 on v0

--- a/solution.py
+++ b/solution.py
@@ -1,6 +1,9 @@
+import functools
 import jax
 import jax.numpy as jnp
 from jax import lax
+from jax.experimental import pallas as pl
+from jax.experimental.pallas import tpu as pltpu
 from jax.sharding import PartitionSpec as P
 
 STEPS = 2
@@ -8,6 +11,341 @@
 
 learn_rate = 2.0
 shrink = 0.02
+decay = 1.0 - learn_rate * shrink
+BF16 = jnp.bfloat16
+F32 = jnp.float32
+NN = (((1,), (0,)), ((), ()))
+NT = (((1,), (1,)), ((), ()))
+
+
+def dot(a, b, dims=NN, precision=None):
+    return lax.dot_general(a, b, dims, precision=precision, preferred_element_type=F32)
+
+
+def split(a):
+    high = a.astype(BF16)
+    return high, (a - high.astype(F32)).astype(BF16)
+
+
+def site_of(shape, axis, states):
+    position = lax.broadcasted_iota(jnp.int32, shape, axis).astype(F32)
+    return jnp.floor((position + 0.5) * (1.0 / states))
+
+
+def same_site(width, states):
+    return (
+        site_of((width, width), 0, states) == site_of((width, width), 1, states)
+    ).astype(F32)
+
+
+def state_of(width, states):
+    position = lax.broadcasted_iota(jnp.int32, (1, width), 1).astype(F32)
+    return position - states * site_of((1, width), 1, states)
+
+
+def field_select(own_sites, states, width):
+    level = lax.broadcasted_iota(jnp.int32, (states, width), 0).astype(F32)
+    select = (level == state_of(width, states)).astype(F32)
+    site = lax.broadcasted_iota(jnp.int32, (own_sites, width), 0).astype(F32)
+    place = (site == site_of((own_sites, width), 1, states)).astype(F32)
+    return select, place
+
+
+def start_blocks(rows_of, slots, coupl_ref, held_ref, sem, width):
+    copies = {}
+    for near, far, source_row, source_col in rows_of:
+        copy = pltpu.make_async_copy(
+            coupl_ref.at[pl.ds(source_row * width, width), 0, source_col, :],
+            held_ref.at[near, far],
+            sem.at[near, far],
+        )
+        copy.start()
+        copies[near, far] = copy
+    return copies
+
+
+def exchange_kernel(
+    sizes,
+    seq_ref, weight_ref, field_ref, coupl_ref,
+    resid_col_ref, resid_row_ref, onehot_col_ref, onehot_row_ref, field_out_ref,
+    held, narrow, onehot, send_d, recv_d, send_t, recv_t,
+    near_send, near_recv, far_send, far_recv,
+    load_sem, d_send, d_recv, t_send, t_recv, near_s, near_r, far_s, far_r,
+    row_s, row_r, col_s, col_r,
+):
+    row_count, col_count, own_sites, states = sizes
+    width = own_sites * states
+    seq_count, site_count = seq_ref.shape
+    row = lax.axis_index("row")
+    col = lax.axis_index("col")
+    rows = [lax.rem(row + k, row_count) for k in range(row_count)]
+    cols = [lax.rem(col + k, col_count) for k in range(col_count)]
+    order = [
+        (c, r, cols[c], rows[r])
+        for r in list(range(1, row_count)) + [0]
+        for c in range(col_count)
+    ]
+    loads = start_blocks(order, None, coupl_ref, held, load_sem, width)
+
+    barrier = pltpu.get_barrier_semaphore()
+    for k in range(1, row_count):
+        pl.semaphore_signal(barrier, inc=1, device_id={"row": rows[k]}, device_id_type=pl.DeviceIdType.MESH)
+    for k in range(1, col_count):
+        pl.semaphore_signal(barrier, inc=1, device_id={"col": cols[k]}, device_id_type=pl.DeviceIdType.MESH)
+
+    codes = seq_ref[...].astype(F32).astype(BF16)
+    levels = state_of(width, states)
+    site = lax.broadcasted_iota(jnp.int32, (site_count, width), 0)
+    lane_site = site_of((site_count, width), 1, states).astype(jnp.int32)
+
+    def encode(block):
+        pick = (site == lane_site + block * own_sites).astype(F32).astype(BF16)
+        return (dot(codes, pick) == levels).astype(F32)
+
+    blocks = row_count * col_count
+    for block in range(blocks):
+        onehot[block] = encode(block).astype(BF16)
+
+    row_hot = [onehot[row * col_count + cols[c]] for c in range(col_count)]
+    col_hot = [onehot[rows[r] * col_count + col] for r in range(row_count)]
+    own_hot = row_hot[0]
+    own_mask = same_site(width, states)
+
+    def remote(source, target, send, receive, place):
+        copy = pltpu.make_async_remote_copy(
+            src_ref=source, dst_ref=target, send_sem=send, recv_sem=receive,
+            device_id=place, device_id_type=pl.DeviceIdType.MESH,
+        )
+        copy.start()
+        return copy
+
+    pl.semaphore_wait(barrier, row_count + col_count - 2)
+    copies = []
+    direct = None
+    for r in list(range(1, row_count)) + [0]:
+        total = None
+        for c in range(col_count):
+            loads[c, r].wait()
+            value = held[c, r]
+            if c == 0 and r == 0:
+                value = value * (1.0 - own_mask)
+            value = value.astype(BF16)
+            narrow[c, r] = value
+            part = dot(row_hot[c], value)
+            total = part if total is None else total + part
+        if r:
+            send_d[r - 1] = total.astype(BF16)
+            copies.append(remote(
+                send_d.at[r - 1], recv_d.at[r - 1], d_send.at[r - 1], d_recv.at[r - 1], {"row": rows[r]}
+            ))
+        else:
+            direct = total
+    transposed = None
+    for c in list(range(1, col_count)) + [0]:
+        total = None
+        for r in range(row_count):
+            part = dot(col_hot[r], narrow[c, r], NT)
+            total = part if total is None else total + part
+        if c:
+            send_t[c - 1] = total.astype(BF16)
+            copies.append(remote(
+                send_t.at[c - 1], recv_t.at[c - 1], t_send.at[c - 1], t_recv.at[c - 1], {"col": cols[c]}
+            ))
+        else:
+            transposed = total
+
+    gram = jnp.zeros((seq_count, seq_count), F32)
+    for block in range(blocks):
+        gram += dot(onehot[block], onehot[block], NT)
+    gram = split(gram)
+    for r in range(row_count):
+        onehot_col_ref[r] = onehot[r * col_count + col]
+    for c in range(col_count):
+        onehot_row_ref[c, 0:width] = onehot[row * col_count + c].astype(F32).T.astype(BF16)
+    own_hot_t = own_hot.astype(F32).T.astype(BF16)
+    own_f32 = own_hot.astype(F32)
+    mask16 = own_mask.astype(BF16)
+    weight_row = weight_ref[...]
+    weight_total = jnp.sum(weight_row)
+    diagonal = lax.broadcasted_iota(jnp.int32, (seq_count, seq_count), 0) == lax.broadcasted_iota(
+        jnp.int32, (seq_count, seq_count), 1
+    )
+    weights = jnp.sum(jnp.where(diagonal, weight_row, 0.0), axis=1, keepdims=True)
+    rate = learn_rate / weight_total
+    select, place = field_select(own_sites, states, width)
+    fields = jnp.sum(
+        dot(field_ref[...], select, precision=lax.Precision.HIGHEST) * place, axis=0, keepdims=True
+    )
+
+    def residual(logits):
+        powers = jnp.exp(logits)
+        high, low = split(powers)
+        sums = dot(high, mask16) + dot(low, mask16)
+        return (weights * (powers / sums - own_f32)).astype(BF16)
+
+    for copy in copies:
+        copy.wait()
+    logits = direct + transposed
+    for k in range(row_count - 1):
+        logits += recv_d[k].astype(F32)
+    for k in range(col_count - 1):
+        logits += recv_t[k].astype(F32)
+    first = residual(logits + fields)
+
+    cross = dot(own_hot, first, NT)
+    near_send[...] = cross.astype(near_send.dtype)
+    copies = [
+        remote(near_send, near_recv.at[c - 1], near_s.at[c - 1], near_r.at[c - 1], {"col": cols[c]})
+        for c in range(1, col_count)
+    ]
+    pairs = split(dot(own_hot_t, first) * own_mask)
+    own_part = sum(dot(own_hot, half) + dot(own_hot, half, NT) for half in pairs)
+    change = dot(gram[0], first) - own_part
+    if site_count > 256:
+        change += dot(gram[1], first)
+    first_wide = first.astype(F32)
+    fields = decay * fields - rate * jnp.sum(first_wide, axis=0, keepdims=True)
+    base = fields + decay * logits - (2.0 * rate) * change
+    for copy in copies:
+        copy.wait()
+    for k in range(col_count - 1):
+        cross += near_recv[k].astype(F32)
+    far_send[...] = cross.astype(far_send.dtype)
+    copies = [
+        remote(far_send, far_recv.at[r - 1], far_s.at[r - 1], far_r.at[r - 1], {"row": rows[r]})
+        for r in range(1, row_count)
+    ]
+    for copy in copies:
+        copy.wait()
+    for k in range(row_count - 1):
+        cross += far_recv[k].astype(F32)
+    cross = split(cross)
+    logits = base - (2.0 * rate) * (dot(cross[0], own_hot) + dot(cross[1], own_hot))
+    second = residual(logits).astype(F32)
+    both = decay * first_wide + second
+    resid_col_ref[row] = both.astype(BF16)
+    copies = [
+        remote(resid_col_ref.at[row], resid_col_ref.at[row], row_s.at[r - 1], row_r.at[r - 1], {"row": rows[r]})
+        for r in range(1, row_count)
+    ]
+    resid_row_ref[col, 0:width] = both.T.astype(BF16)
+    if resid_row_ref.shape[1] > width:
+        pad = resid_row_ref.shape[1] - width
+        resid_row_ref[col, width:] = jnp.zeros((pad, seq_count), BF16)
+    copies += [
+        remote(resid_row_ref.at[col], resid_row_ref.at[col], col_s.at[c - 1], col_r.at[c - 1], {"col": cols[c]})
+        for c in range(1, col_count)
+    ]
+    field_out_ref[...] = decay * fields - rate * jnp.sum(second, axis=0, keepdims=True)
+    for copy in copies:
+        copy.wait()
+
+
+def update_kernel(
+    sizes,
+    weight_ref, field_ref, resid_col_ref, resid_row_ref, onehot_col_ref, onehot_row_ref, coupl_ref,
+    out_ref, field_out_ref,
+    held, load_sem, store_sem,
+):
+    row_count, col_count, own_sites, states = sizes
+    width = own_sites * states
+    row = lax.axis_index("row")
+    col = lax.axis_index("col")
+    rows = [lax.rem(row + k, row_count) for k in range(row_count)]
+    cols = [lax.rem(col + k, col_count) for k in range(col_count)]
+    order = [(c, r, cols[c], rows[r]) for c in range(col_count) for r in range(row_count)]
+    loads = start_blocks(order, None, coupl_ref, held, load_sem, width)
+    rate = learn_rate / jnp.sum(weight_ref[...])
+    select, place = field_select(own_sites, states, width)
+    field_out_ref[...] = dot(
+        field_ref[...] * place, select, NT, precision=lax.Precision.HIGHEST
+    )
+    stores = []
+    for c, r, source_row, source_col in order:
+        left = jnp.concatenate(
+            [onehot_row_ref[source_row, 0:width], resid_row_ref[source_row, 0:width]], axis=1
+        )
+        right = jnp.concatenate([resid_col_ref[source_col], onehot_col_ref[source_col]], axis=0)
+        grad = dot(left, right)
+        loads[c, r].wait()
+        value = (decay * decay) * held[c, r] - rate * grad
+        if c == 0 and r == 0:
+            value = value * (1.0 - same_site(width, states))
+        held[c, r] = value
+        copy = pltpu.make_async_copy(
+            held.at[c, r],
+            out_ref.at[pl.ds(source_row * width, width), 0, source_col, :],
+            store_sem.at[c, r],
+        )
+        copy.start()
+        stores.append(copy)
+    for copy in stores:
+        copy.wait()
+
+
+def fused_device(sequences, seq_weights, fields, couplings):
+    row_count, col_count = lax.axis_size("row"), lax.axis_size("col")
+    own_sites, states = fields.shape
+    width = own_sites * states
+    padded = -(-width // 16) * 16
+    seq_count = sequences.shape[0]
+    sizes = (row_count, col_count, own_sites, states)
+    weights = seq_weights.reshape(1, seq_count)
+    vmem = pl.BlockSpec(memory_space=pltpu.VMEM)
+    hbm = pl.BlockSpec(memory_space=pl.ANY)
+    dma = pltpu.SemaphoreType.DMA
+    row_more, col_more = row_count - 1, col_count - 1
+    square = (seq_count, seq_count)
+    flat = (seq_count, width)
+    resid_col, resid_row, onehot_col, onehot_row, field_flat = pl.pallas_call(
+        functools.partial(exchange_kernel, sizes),
+        out_shape=[
+            jax.ShapeDtypeStruct((row_count, seq_count, width), BF16),
+            jax.ShapeDtypeStruct((col_count, padded, seq_count), BF16),
+            jax.ShapeDtypeStruct((row_count, seq_count, width), BF16),
+            jax.ShapeDtypeStruct((col_count, padded, seq_count), BF16),
+            jax.ShapeDtypeStruct((1, width), F32),
+        ],
+        in_specs=[vmem, vmem, vmem, hbm],
+        out_specs=[vmem] * 5,
+        scratch_shapes=[
+            pltpu.VMEM((col_count, row_count, width, width), F32),
+            pltpu.VMEM((col_count, row_count, width, width), BF16),
+            pltpu.VMEM((row_count * col_count,) + flat, BF16),
+            pltpu.VMEM((row_more,) + flat, BF16),
+            pltpu.VMEM((row_more,) + flat, BF16),
+            pltpu.VMEM((col_more,) + flat, BF16),
+            pltpu.VMEM((col_more,) + flat, BF16),
+            pltpu.VMEM(square, F32),
+            pltpu.VMEM((col_more,) + square, F32),
+            pltpu.VMEM(square, F32),
+            pltpu.VMEM((row_more,) + square, F32),
+            dma((col_count, row_count)),
+            dma((row_more,)), dma((row_more,)), dma((col_more,)), dma((col_more,)),
+            dma((col_more,)), dma((col_more,)), dma((row_more,)), dma((row_more,)),
+            dma((row_more,)), dma((row_more,)), dma((col_more,)), dma((col_more,)),
+        ],
+        compiler_params=pltpu.CompilerParams(
+            collective_id=0, has_side_effects=True, vmem_limit_bytes=40 * 1024 * 1024
+        ),
+        name="exchange",
+    )(sequences, weights, fields, couplings)
+    return pl.pallas_call(
+        functools.partial(update_kernel, sizes),
+        out_shape=[
+            jax.ShapeDtypeStruct(couplings.shape, F32),
+            jax.ShapeDtypeStruct(fields.shape, F32),
+        ],
+        in_specs=[vmem] * 6 + [hbm],
+        out_specs=[hbm, vmem],
+        scratch_shapes=[
+            pltpu.VMEM((col_count, row_count, width, width), F32),
+            dma((col_count, row_count)),
+            dma((col_count, row_count)),
+        ],
+        compiler_params=pltpu.CompilerParams(vmem_limit_bytes=40 * 1024 * 1024),
+        name="update",
+    )(weights, field_flat, resid_col, resid_row, onehot_col, onehot_row, couplings)
 
 
 def per_device(sequences, seq_weights, fields, couplings):
@@ -110,6 +448,7 @@
         P(("groups", "row", "rep"), "col", None, None),
     )
     out_specs = (P(("groups", "row", "rep"), "col", None, None), P(("groups", "row", "col"), None))
+    fused = mesh.shape["rep"] == 1 and mesh.shape["row"] > 1 and mesh.shape["col"] > 1
     return jax.shard_map(
-        per_device, mesh=mesh, in_specs=in_specs, out_specs=out_specs, check_vma=False
-    )
+        fused_device if fused else per_device, mesh=mesh, in_specs=in_specs, out_specs=out_specs, check_vma=False
+    )

time: 158 us -> 59 us (0.37)
  blocking collectives: 90.6 us -> 0 us
  Pallas kernels: 0 us -> 43 us
  other arithmetic: 20.2 us -> 0 us
  matrix products: 13.5 us -> 0 us
  local copies, waits for them, and re-layouts: 23.9 us -> 14.9 us
  starting transfers between devices: 6.23 us -> 0 us
  between operations: 2.53 us -> 0.7 us
    unnamed x4 -> x0, blocking collectives: 47.1 us -> none
    all_gather x4 -> x0, blocking collectives: 43.5 us -> none  [the longest x2 29.2 us: per_device(): by_row = lax.all_gather(all_resid, 'row', axis=0, tiled=True)]
    pallas_call x0 -> x2, Pallas kernels: none -> 43 us  [the longest x1 33.4 us: fused_device(): pl.pallas_call(functools.partial(exchange_kernel, sizes), out_shape=[jax....]
    dot_general x8 -> x0, matrix products: 13.5 us -> none  [the longest x2 4.51 us: per_device(): lax.dot_general(mine_rows, wide_col, (((1,), (0,)), ((), ())), preferred_...]
    convert_element_type x2 -> x0, other arithmetic: 6.83 us -> none  [per_device(): coupl.reshape(half_rows, row_count * block_width).astype(jnp.bfloat16)]
    reshape x5 -> x0, local copies, waits for them, and re-layouts: 6.72 us -> none  [the longest x2 6.04 us: per_device(): coupling_grad = coupling_grad.reshape(half_rows, 1, row_count, block_width)]
    unnamed x4 -> x0, starting transfers between devices: 6.23 us -> none
    pallas_call x0 -> x1, local copies, waits for them, and re-layouts: none -> 5.71 us  [fused_device(): pl.pallas_call(functools.partial(update_kernel, sizes), out_shape=[jax.Sh...]
  transfers between devices with their start and end apart: 4 -> 0, of which waited for: 0 -> 0; matrix products, arithmetic and copies ran while one was open for 9% -> 0% of each run, Pallas kernels for 0% -> 0%
where the time goes in v1:
time: 59 us; the launch traced here: 58.6 us
  Pallas kernels  43 us (73%)
  local copies, waits for them, and re-layouts  14.9 us (25%)
  between operations  0.7 us (1%)
    pallas_call x1, Pallas kernels, fused_device(): pl.pallas_call(functools.partial(exchange_kernel, sizes), out_shape=[jax....  33.4 us
    pallas_call x1, Pallas kernels, fused_device(): pl.pallas_call(functools.partial(update_kernel, sizes), out_shape=[jax.Sh...  9.56 us
    unnamed x10, local copies, waits for them, and re-layouts  9.21 us
    pallas_call x1, local copies, waits for them, and re-layouts, fused_device(): pl.pallas_call(functools.partial(update_kernel, sizes), out_shape=[jax.Sh...  5.71 us

profile of v1, /device:TPU:0, one launch (start us, length us, event | category | flops | bytes accessed | tf_op | source)
XLA Modules:
  0.0 58.6 jit_solution(15897434953037360046)
XLA Ops:
  0.6 0.0 copy-start.2
  0.6 0.0 copy-start.3
  0.6 1.7 %copy.6.seq_ref = s32[128,160]{1,0:T(8,128)} copy(s32[128,160]{0,1:T(8,128)} %param.4) | data formatting | bytes 163840 | tf_op args[0]
  2.3 4.9 %copy.7.coupl_ref = f32[840,1,4,210]{3,2,1,0:T(4,128)S(1)} copy(f32[840,1,4,210]{0,2,3,1:T(4,128)} %param.7) | data formatting | bytes 5644800 | tf_op args[3]
  7.2 0.0 copy-done.2
  7.3 0.0 copy-done.3
  7.3 0.0 copy-start.1
  7.3 0.9 %copy-done.1 = s32[128,160]{1,0:T(8,128)S(1)} copy-done((s32[128,160]{1,0:T(8,128)S(1)}, s32[128,160]{1,0:T(8,128)}, u32[]{:S(2)}) %copy-start.1) | copy-done | bytes 81944
  8.2 33.4 %exchange.1 = (bf16[4,128,210]{2,1,0:T(8,128)(2,1)S(1)}, bf16[4,224,128]{2,1,0:T(8,128)(2,1)S(1)}, bf16[4,128,210]{2,1,0:T(8,128)(2,1)S(1)}, bf16[4,224,128]{2,1,0:T(8,128)(2,1)S(1)}, f32[1,210]{1,0:T(1,128)S(1)}) custom-call(s32[128,160]{1,0:T(8,128)S(1)} %copy-done.1, f32[1,128]{1,0:T(1,128)S(1)} %bitcast.1, f32[10,21]{1,0:T(8,128)S(1)} %copy-done.2, ...), custom_call_target="tpu_custom_call" | custom-call | tf_op jit(solution)/shard_map/exchange/pallas_call | solution.py:300
  41.6 9.6 %update.1 = (f32[840,1,4,210]{3,2,1,0:T(4,128)S(1)}, f32[10,21]{1,0:T(8,128)}) custom-call(f32[1,128]{1,0:T(1,128)S(1)} %bitcast.2, f32[1,210]{1,0:T(1,128)S(1)} %get-tuple-element.7.field_ref, bf16[4,128,210]{2,1,0:T(8,128)(2,1)S(1)} %get-tuple-element.8.resid_col_ref, bf16[4,224,128]{2,1,0:T(8,128)(2,1)S(1)} %get-tuple-element.9.resid_row_ref, ...), custom_call_target="tpu_custom_call" | custom-call | tf_op jit(solution)/shard_map/update/pallas_call | solution.py:333
  51.2 0.0 copy-start
  51.2 1.7 %copy-done = f32[840,1,4,210]{3,2,1,0:T(4,128)} copy-done((f32[840,1,4,210]{3,2,1,0:T(4,128)}, f32[840,1,4,210]{3,2,1,0:T(4,128)S(1)}, u32[]{:S(2)}) %copy-start) | copy-done | bytes 2822424
  52.9 5.7 %copy.9 = f32[840,1,4,210]{0,2,3,1:T(4,128)} copy(f32[840,1,4,210]{3,2,1,0:T(4,128)} %copy-done) | data formatting | bytes 5644800 | tf_op jit(solution)/shard_map/update/pallas_call | solution.py:333
Async XLA Ops:
  0.6 6.6 %copy-start.2 = (f32[10,21]{1,0:T(8,128)S(1)}, f32[10,21]{1,0:T(8,128)}, u32[]{:S(2)}) copy-start(f32[10,21]{1,0:T(8,128)} %field_ref.1) | copy-start | bytes 2524
  0.6 6.6 %copy-start.3 = (f32[128]{0:T(128)S(1)}, f32[128]{0:T(128)}, u32[]{:S(2)}) copy-start(f32[128]{0:T(128)} %param.5) | copy-start | bytes 1540
  7.3 0.9 %copy-start.1 = (s32[128,160]{1,0:T(8,128)S(1)}, s32[128,160]{1,0:T(8,128)}, u32[]{:S(2)}) copy-start(s32[128,160]{1,0:T(8,128)} %copy.6.seq_ref) | copy-start | bytes 245764
  51.2 1.7 %copy-start = (f32[840,1,4,210]{3,2,1,0:T(4,128)}, f32[840,1,4,210]{3,2,1,0:T(4,128)S(1)}, u32[]{:S(2)}) copy-start(f32[840,1,4,210]{3,2,1,0:T(4,128)S(1)} %get-tuple-element.12) | copy-start | bytes 8467204

commit v2 on v0

--- a/solution.py
+++ b/solution.py
@@ -1,6 +1,9 @@
+import functools
 import jax
 import jax.numpy as jnp
 from jax import lax
+from jax.experimental import pallas as pl
+from jax.experimental.pallas import tpu as pltpu
 from jax.sharding import PartitionSpec as P
 
 STEPS = 2
@@ -8,6 +11,376 @@
 
 learn_rate = 2.0
 shrink = 0.02
+decay = 1.0 - learn_rate * shrink
+BF16 = jnp.bfloat16
+F32 = jnp.float32
+CROSS = jnp.bfloat16
+NN = (((1,), (0,)), ((), ()))
+
+
+def dot(a, b, dims=NN, precision=None):
+    return lax.dot_general(a, b, dims, precision=precision, preferred_element_type=F32)
+
+
+def split(a):
+    high = a.astype(BF16)
+    return high, (a - high.astype(F32)).astype(BF16)
+
+
+def site_of(shape, axis, states):
+    position = lax.broadcasted_iota(jnp.int32, shape, axis).astype(F32)
+    return jnp.floor((position + 0.5) * (1.0 / states))
+
+
+def state_of(shape, axis, states):
+    position = lax.broadcasted_iota(jnp.int32, shape, axis).astype(F32)
+    return position - states * site_of(shape, axis, states)
+
+
+def same_site(width, states):
+    shape = (width, width)
+    return (site_of(shape, 0, states) == site_of(shape, 1, states)).astype(F32)
+
+
+def diagonal_part(shape, col, own_sites, states):
+    offset = (col * own_sites).astype(F32)
+    return (site_of(shape, 0, states) + offset != site_of(shape, 1, states)).astype(F32)
+
+
+def field_select(own_sites, states, width):
+    level = lax.broadcasted_iota(jnp.int32, (width, states), 1).astype(F32)
+    select = (level == state_of((width, states), 0, states)).astype(F32)
+    site = lax.broadcasted_iota(jnp.int32, (width, own_sites), 1).astype(F32)
+    place = (site == site_of((width, own_sites), 0, states)).astype(F32)
+    return select, place
+
+
+def encode_wide(codes_t, first_site, length, states):
+    sites = codes_t.shape[0]
+    shape = (length, sites)
+    wanted = site_of(shape, 0, states).astype(jnp.int32) + first_site
+    pick = (lax.broadcasted_iota(jnp.int32, shape, 1) == wanted).astype(F32).astype(BF16)
+    level = state_of((length, 1), 0, states)
+    return (dot(pick, codes_t) == level).astype(F32).astype(BF16)
+
+
+def encode_tall(codes, first_site, length, states):
+    sites = codes.shape[1]
+    shape = (sites, length)
+    wanted = site_of(shape, 1, states).astype(jnp.int32) + first_site
+    pick = (lax.broadcasted_iota(jnp.int32, shape, 0) == wanted).astype(F32).astype(BF16)
+    level = state_of((1, length), 1, states)
+    return (dot(codes, pick) == level).astype(F32).astype(BF16)
+
+
+def start_blocks(row_count, rows, coupl_ref, held_ref, sem):
+    copies = {}
+    for k in list(range(1, row_count)) + [0]:
+        copy = pltpu.make_async_copy(coupl_ref.at[0, :, rows[k], :], held_ref.at[k], sem.at[k])
+        copy.start()
+        copies[k] = copy
+    return copies
+
+
+def exchange_kernel(
+    sizes,
+    seq_ref, weight_ref, field_ref, coupl_ref,
+    held, first_col_ref, first_row_ref, second_col_ref, second_row_ref, onehot_col_ref, onehot_row_ref,
+    field_out_ref,
+    turned, own_t, send_d, recv_d, send_t, recv_t, first_own, second_own,
+    near_send, near_recv, far_send, far_recv,
+    load_sem, d_send, d_recv, t_send, t_recv, near_s, near_r, far_s, far_r,
+    first_row_s, first_row_r, first_col_s, first_col_r,
+    second_row_s, second_row_r, second_col_s, second_col_r,
+):
+    row_count, col_count, own_sites, states = sizes
+    width = own_sites * states
+    wide = width * col_count
+    site_count, seq_count = seq_ref.shape
+    row = lax.axis_index("row")
+    col = lax.axis_index("col")
+    rows = [lax.rem(row + k, row_count) for k in range(row_count)]
+    cols = [lax.rem(col + k, col_count) for k in range(col_count)]
+    loads = start_blocks(row_count, rows, coupl_ref, held, load_sem)
+
+    mesh_id = pl.DeviceIdType.MESH
+    barrier = pltpu.get_barrier_semaphore()
+    for k in range(1, row_count):
+        pl.semaphore_signal(barrier, inc=1, device_id={"row": rows[k]}, device_id_type=mesh_id)
+    for k in range(1, col_count):
+        pl.semaphore_signal(barrier, inc=1, device_id={"col": cols[k]}, device_id_type=mesh_id)
+
+    def remote(source, target, send, receive, place):
+        copy = pltpu.make_async_remote_copy(
+            src_ref=source, dst_ref=target, send_sem=send, recv_sem=receive,
+            device_id=place, device_id_type=mesh_id,
+        )
+        copy.start()
+        return copy
+
+    padded = send_d.shape[1]
+    if padded > width:
+        pad = padded - width
+        for k in range(row_count - 1):
+            send_d[k, width:] = jnp.zeros((pad, seq_count), BF16)
+        for k in range(col_count):
+            send_t[k, width:] = jnp.zeros((pad, seq_count), BF16)
+        first_own[width:] = jnp.zeros((pad, seq_count), BF16)
+        second_own[width:] = jnp.zeros((pad, seq_count), BF16)
+    codes_f32 = seq_ref[...].astype(F32)
+    codes_t = codes_f32.astype(BF16)
+    codes = codes_f32.T.astype(BF16)
+    row_hot_t = encode_wide(codes_t, row * (col_count * own_sites), wide, states)
+    col_hot = [
+        encode_tall(codes, (rows[k] * col_count + col) * own_sites, width, states)
+        for k in range(row_count)
+    ]
+    apart = diagonal_part((width, wide), col, own_sites, states)
+
+    pl.semaphore_wait(barrier, row_count + col_count - 2)
+    copies = []
+    direct = None
+    tall = None
+    for k in list(range(1, row_count)) + [0]:
+        loads[k].wait()
+        value = held[k]
+        if k == 0:
+            value = value * apart
+            held[k] = value
+        value = value.astype(BF16)
+        part = dot(value, row_hot_t)
+        if k:
+            send_d[k - 1, 0:width] = part.astype(BF16)
+            copies.append(remote(
+                send_d.at[k - 1], recv_d.at[k - 1], d_send.at[k - 1], d_recv.at[k - 1], {"row": rows[k]}
+            ))
+        else:
+            direct = part
+        part = dot(col_hot[k], value)
+        tall = part if tall is None else tall + part
+    turned[...] = tall.T
+    for c in range(col_count):
+        block = turned[c * width : (c + 1) * width]
+        own_t[c, 0:width] = block
+        send_t[c, 0:width] = block.astype(BF16)
+    for k in range(1, col_count):
+        copies.append(remote(
+            send_t.at[cols[k]], recv_t.at[k - 1], t_send.at[k - 1], t_recv.at[k - 1], {"col": cols[k]}
+        ))
+
+    gram = jnp.zeros((seq_count, seq_count), F32)
+    for level in range(states):
+        left = (codes.astype(F32) == level).astype(F32).astype(BF16)
+        right = (codes_f32 == level).astype(F32).astype(BF16)
+        gram += dot(left, right)
+    gram = split(gram)
+    for r in range(row_count):
+        onehot_col_ref[r, 0:width] = encode_wide(
+            codes_t, (r * col_count + col) * own_sites, width, states
+        )
+    onehot_row_ref[...] = encode_tall(codes, row * (col_count * own_sites), wide, states)
+    own_hot = col_hot[0]
+    own_hot_t = encode_wide(codes_t, (row * col_count + col) * own_sites, width, states)
+    own_f32 = own_hot_t.astype(F32)
+    own_mask = same_site(width, states)
+    mask16 = own_mask.astype(BF16)
+    weights = weight_ref[...]
+    rate = learn_rate / jnp.sum(weights)
+    select, place = field_select(own_sites, states, width)
+    fields = jnp.sum(
+        dot(place, field_ref[...], precision=lax.Precision.HIGHEST) * select, axis=1, keepdims=True
+    )
+
+    def residual(logits):
+        powers = jnp.exp(logits)
+        high, low = split(powers)
+        sums = dot(mask16, high) + dot(mask16, low)
+        return weights * (powers / sums - own_f32)
+
+    for copy in copies:
+        copy.wait()
+    logits = direct + own_t[col, 0:width]
+    for k in range(row_count - 1):
+        logits += recv_d[k, 0:width].astype(F32)
+    for k in range(col_count - 1):
+        logits += recv_t[k, 0:width].astype(F32)
+    first = residual(logits + fields).astype(BF16)
+    first_own[0:width] = first
+    first_wide = first.astype(F32)
+    first_tall = first_wide.T.astype(BF16)
+
+    cross = dot(first_tall, own_hot_t)
+    near_send[...] = cross.astype(near_send.dtype)
+    copies = [
+        remote(near_send, near_recv.at[k - 1], near_s.at[k - 1], near_r.at[k - 1], {"col": cols[k]})
+        for k in range(1, col_count)
+    ]
+    pairs = split((dot(own_hot_t, first_tall) + dot(first, own_hot)) * own_mask)
+    change = dot(first, gram[0]) - dot(pairs[0], own_hot_t) - dot(pairs[1], own_hot_t)
+    if site_count > 256:
+        change += dot(first, gram[1])
+    fields = decay * fields - rate * jnp.sum(first_wide, axis=1, keepdims=True)
+    base = fields + decay * logits - (2.0 * rate) * change
+    for copy in copies:
+        copy.wait()
+    for k in range(col_count - 1):
+        cross += near_recv[k].astype(F32)
+    far_send[...] = cross.astype(far_send.dtype)
+    copies = [
+        remote(far_send, far_recv.at[k - 1], far_s.at[k - 1], far_r.at[k - 1], {"row": rows[k]})
+        for k in range(1, row_count)
+    ]
+    far_copies = copies
+    copies = [
+        remote(first_own, first_row_ref.at[col], first_col_s.at[k - 1], first_col_r.at[k - 1], {"col": cols[k]})
+        for k in range(1, col_count)
+    ]
+    for copy in far_copies:
+        copy.wait()
+    copies += [
+        remote(first_own, first_col_ref.at[row], first_row_s.at[k - 1], first_row_r.at[k - 1], {"row": rows[k]})
+        for k in range(1, row_count)
+    ]
+    for k in range(row_count - 1):
+        cross += far_recv[k].astype(F32)
+    cross = split(cross)
+    logits = base - (2.0 * rate) * (dot(own_hot_t, cross[0]) + dot(own_hot_t, cross[1]))
+    second = residual(logits).astype(BF16)
+    second_own[0:width] = second
+    second = second.astype(F32)
+    copies += [
+        remote(second_own, second_col_ref.at[row], second_row_s.at[k - 1], second_row_r.at[k - 1], {"row": rows[k]})
+        for k in range(1, row_count)
+    ]
+    copies += [
+        remote(second_own, second_row_ref.at[col], second_col_s.at[k - 1], second_col_r.at[k - 1], {"col": cols[k]})
+        for k in range(1, col_count)
+    ]
+    for own_ref, by_col, by_row in (
+        (first_own, first_col_ref, first_row_ref), (second_own, second_col_ref, second_row_ref)
+    ):
+        own = own_ref[...]
+        by_col[row] = own
+        by_row[col] = own
+    field_out_ref[...] = decay * fields - rate * jnp.sum(second, axis=1, keepdims=True)
+    for copy in copies:
+        copy.wait()
+
+
+def update_kernel(
+    sizes,
+    weight_ref, field_ref, held_ref, first_col_ref, first_row_ref, second_col_ref, second_row_ref,
+    onehot_col_ref, onehot_row_ref,
+    out_ref, field_out_ref,
+    result, stacked, store_sem,
+):
+    row_count, col_count, own_sites, states = sizes
+    width = own_sites * states
+    wide = width * col_count
+    row = lax.axis_index("row")
+    col = lax.axis_index("col")
+    rows = [lax.rem(row + k, row_count) for k in range(row_count)]
+    rate = learn_rate / jnp.sum(weight_ref[...])
+    select, place = field_select(own_sites, states, width)
+    field_out_ref[...] = lax.dot_general(
+        place, field_ref[...] * select, (((0,), (0,)), ((), ())),
+        precision=lax.Precision.HIGHEST, preferred_element_type=F32,
+    )
+    rights = []
+    for by_row in (first_row_ref, second_row_ref):
+        for c in range(col_count):
+            stacked[c * width : (c + 1) * width] = by_row[c, 0:width].astype(F32)
+        rights.append(jnp.concatenate([stacked[...].T.astype(BF16), onehot_row_ref[...]], axis=0))
+    stores = []
+    for k in range(row_count):
+        value = (decay * decay) * held_ref[k]
+        hot = onehot_col_ref[rows[k], 0:width]
+        for by_col, right, scale in (
+            (first_col_ref, rights[0], decay), (second_col_ref, rights[1], 1.0)
+        ):
+            left = jnp.concatenate([hot, by_col[rows[k], 0:width]], axis=1)
+            value = value - (scale * rate) * dot(left, right)
+        if k == 0:
+            value = value * diagonal_part((width, wide), col, own_sites, states)
+        result[k] = value
+        copy = pltpu.make_async_copy(result.at[k], out_ref.at[0, :, rows[k], :], store_sem.at[k])
+        copy.start()
+        stores.append(copy)
+    for copy in stores:
+        copy.wait()
+
+
+def fused_device(sequences, seq_weights, fields, couplings):
+    row_count, col_count = lax.axis_size("row"), lax.axis_size("col")
+    own_sites, states = fields.shape
+    width = own_sites * states
+    wide = width * col_count
+    padded = -(-width // 16) * 16
+    seq_count = sequences.shape[0]
+    sizes = (row_count, col_count, own_sites, states)
+    weights = seq_weights.reshape(1, seq_count)
+    turned = couplings.transpose(1, 3, 2, 0)
+    vmem = pl.BlockSpec(memory_space=pltpu.VMEM)
+    hbm = pl.BlockSpec(memory_space=pltpu.HBM)
+    dma = pltpu.SemaphoreType.DMA
+    row_more, col_more = row_count - 1, col_count - 1
+    square = (seq_count, seq_count)
+    flat = (padded, seq_count)
+    held, *parts, field_flat = pl.pallas_call(
+        functools.partial(exchange_kernel, sizes),
+        out_shape=[
+            jax.ShapeDtypeStruct((row_count, width, wide), F32),
+            jax.ShapeDtypeStruct((row_count,) + flat, BF16),
+            jax.ShapeDtypeStruct((col_count,) + flat, BF16),
+            jax.ShapeDtypeStruct((row_count,) + flat, BF16),
+            jax.ShapeDtypeStruct((col_count,) + flat, BF16),
+            jax.ShapeDtypeStruct((row_count,) + flat, BF16),
+            jax.ShapeDtypeStruct((seq_count, wide), BF16),
+            jax.ShapeDtypeStruct((width, 1), F32),
+        ],
+        in_specs=[vmem, vmem, vmem, hbm],
+        out_specs=[vmem] * 8,
+        scratch_shapes=[
+            pltpu.VMEM((wide, seq_count), F32),
+            pltpu.VMEM((col_count,) + flat, F32),
+            pltpu.VMEM((row_more,) + flat, BF16),
+            pltpu.VMEM((row_more,) + flat, BF16),
+            pltpu.VMEM((col_count,) + flat, BF16),
+            pltpu.VMEM((col_more,) + flat, BF16),
+            pltpu.VMEM(flat, BF16),
+            pltpu.VMEM(flat, BF16),
+            pltpu.VMEM(square, CROSS),
+            pltpu.VMEM((col_more,) + square, CROSS),
+            pltpu.VMEM(square, CROSS),
+            pltpu.VMEM((row_more,) + square, CROSS),
+            dma((row_count,)),
+            dma((row_more,)), dma((row_more,)), dma((col_more,)), dma((col_more,)),
+            dma((col_more,)), dma((col_more,)), dma((row_more,)), dma((row_more,)),
+            dma((row_more,)), dma((row_more,)), dma((col_more,)), dma((col_more,)),
+            dma((row_more,)), dma((row_more,)), dma((col_more,)), dma((col_more,)),
+        ],
+        compiler_params=pltpu.CompilerParams(
+            collective_id=0, has_side_effects=True, vmem_limit_bytes=58 * 1024 * 1024
+        ),
+        name="exchange",
+    )(sequences.T, weights, fields, turned)
+    out, new_fields = pl.pallas_call(
+        functools.partial(update_kernel, sizes),
+        out_shape=[
+            jax.ShapeDtypeStruct(turned.shape, F32),
+            jax.ShapeDtypeStruct(fields.shape, F32),
+        ],
+        in_specs=[vmem] * 9,
+        out_specs=[hbm, vmem],
+        scratch_shapes=[
+            pltpu.VMEM((row_count, width, wide), F32),
+            pltpu.VMEM((wide, seq_count), F32),
+            dma((row_count,)),
+        ],
+        compiler_params=pltpu.CompilerParams(vmem_limit_bytes=40 * 1024 * 1024),
+        name="update",
+    )(weights, field_flat, held, *parts)
+    return (out.transpose(3, 0, 2, 1), new_fields)
 
 
 def per_device(sequences, seq_weights, fields, couplings):
@@ -110,6 +483,7 @@
         P(("groups", "row", "rep"), "col", None, None),
     )
     out_specs = (P(("groups", "row", "rep"), "col", None, None), P(("groups", "row", "col"), None))
+    fused = mesh.shape["rep"] == 1 and mesh.shape["row"] > 1 and mesh.shape["col"] > 1
     return jax.shard_map(
-        per_device, mesh=mesh, in_specs=in_specs, out_specs=out_specs, check_vma=False
-    )
+        fused_device if fused else per_device, mesh=mesh, in_specs=in_specs, out_specs=out_specs, check_vma=False
+    )

time: 158 us -> 47.6 us (0.30)
  blocking collectives: 90.6 us -> 0 us
  Pallas kernels: 0 us -> 38.2 us
  other arithmetic: 20.2 us -> 0 us
  local copies, waits for them, and re-layouts: 23.9 us -> 8.4 us
  matrix products: 13.5 us -> 0 us
  starting transfers between devices: 6.23 us -> 0 us
  between operations: 2.53 us -> 0.67 us
    unnamed x4 -> x0, blocking collectives: 47.1 us -> none
    all_gather x4 -> x0, blocking collectives: 43.5 us -> none  [the longest x2 29.2 us: per_device(): by_row = lax.all_gather(all_resid, 'row', axis=0, tiled=True)]
    pallas_call x0 -> x2, Pallas kernels: none -> 38.2 us  [the longest x1 34.7 us: fused_device(): pl.pallas_call(functools.partial(exchange_kernel, sizes), out_shape=[jax....]
    dot_general x8 -> x0, matrix products: 13.5 us -> none  [the longest x2 4.51 us: per_device(): lax.dot_general(mine_rows, wide_col, (((1,), (0,)), ((), ())), preferred_...]
    convert_element_type x2 -> x0, other arithmetic: 6.83 us -> none  [per_device(): coupl.reshape(half_rows, row_count * block_width).astype(jnp.bfloat16)]
    reshape x5 -> x0, local copies, waits for them, and re-layouts: 6.72 us -> none  [the longest x2 6.04 us: per_device(): coupling_grad = coupling_grad.reshape(half_rows, 1, row_count, block_width)]
    unnamed x4 -> x0, starting transfers between devices: 6.23 us -> none
    sub x3 -> x0, other arithmetic: 5.62 us -> none  [the longest x1 4.31 us: per_device(): coupl - learn_rate * (off_diagonal * coupling_grad / weight_total + shrin...]
  transfers between devices with their start and end apart: 4 -> 0, of which waited for: 0 -> 0; matrix products, arithmetic and copies ran while one was open for 9% -> 0% of each run, Pallas kernels for 0% -> 0%
where the time goes in v2:
time: 47.6 us; the launch traced here: 47.2 us
  Pallas kernels  38.2 us (80%)
  local copies, waits for them, and re-layouts  8.4 us (18%)
  between operations  0.67 us (1%)
    pallas_call x1, Pallas kernels, fused_device(): pl.pallas_call(functools.partial(exchange_kernel, sizes), out_shape=[jax....  34.7 us
    unnamed x18, local copies, waits for them, and re-layouts  8.4 us
    pallas_call x1, Pallas kernels, fused_device(): pl.pallas_call(functools.partial(update_kernel, sizes), out_shape=[jax.Sh...  3.48 us

profile of v2, /device:TPU:0, one launch (start us, length us, event | category | flops | bytes accessed | tf_op | source)
XLA Modules:
  0.0 47.2 jit_solution(4621815113310176672)
XLA Ops:
  0.6 0.0 copy-start.8
  0.6 34.7 %exchange.1 = (f32[4,210,840]{2,1,0:T(8,128)}, bf16[4,224,128]{2,1,0:T(8,128)(2,1)}, bf16[4,224,128]{2,1,0:T(8,128)(2,1)}, bf16[4,224,128]{2,1,0:T(8,128)(2,1)},...) custom-call(s32[160,128]{1,0:T(8,128)} %bitcast.7, ...), custom_call_target="tpu_custom_call" | custom-call | tf_op jit(solution)/shard_map/exchange/pallas_call | solution.py:329
  35.3 0.0 copy-done.8
  35.3 0.0 copy-start
  35.4 1.9 %copy-done = f32[4,210,840]{2,1,0:T(8,128)S(1)} copy-done((f32[4,210,840]{2,1,0:T(8,128)S(1)}, f32[4,210,840]{2,1,0:T(8,128)}, u32[]{:S(2)}) %copy-start) | copy-done | bytes 2822424
  37.2 0.0 copy-start.1
  37.2 0.9 %copy-done.1 = bf16[4,224,128]{2,1,0:T(8,128)(2,1)S(1)} copy-done((bf16[4,224,128]{2,1,0:T(8,128)(2,1)S(1)}, bf16[4,224,128]{2,1,0:T(8,128)(2,1)}, u32[]{:S(2)}) %copy-start.1) | copy-done | bytes 229400
  38.2 0.0 copy-start.2
  38.2 0.9 %copy-done.2 = bf16[4,224,128]{2,1,0:T(8,128)(2,1)S(1)} copy-done((bf16[4,224,128]{2,1,0:T(8,128)(2,1)S(1)}, bf16[4,224,128]{2,1,0:T(8,128)(2,1)}, u32[]{:S(2)}) %copy-start.2) | copy-done | bytes 229400
  39.1 0.0 copy-start.3
  39.1 0.9 %copy-done.3 = bf16[4,224,128]{2,1,0:T(8,128)(2,1)S(1)} copy-done((bf16[4,224,128]{2,1,0:T(8,128)(2,1)S(1)}, bf16[4,224,128]{2,1,0:T(8,128)(2,1)}, u32[]{:S(2)}) %copy-start.3) | copy-done | bytes 229400
  40.0 0.0 copy-start.4
  40.0 0.9 %copy-done.4 = bf16[4,224,128]{2,1,0:T(8,128)(2,1)S(1)} copy-done((bf16[4,224,128]{2,1,0:T(8,128)(2,1)S(1)}, bf16[4,224,128]{2,1,0:T(8,128)(2,1)}, u32[]{:S(2)}) %copy-start.4) | copy-done | bytes 229400
  41.0 0.0 copy-start.5
  41.0 0.9 %copy-done.5 = bf16[4,224,128]{2,1,0:T(8,128)(2,1)S(1)} copy-done((bf16[4,224,128]{2,1,0:T(8,128)(2,1)S(1)}, bf16[4,224,128]{2,1,0:T(8,128)(2,1)}, u32[]{:S(2)}) %copy-start.5) | copy-done | bytes 229400
  41.9 0.0 copy-start.6
  41.9 0.9 %copy-done.6 = bf16[128,840]{1,0:T(8,128)(2,1)S(1)} copy-done((bf16[128,840]{1,0:T(8,128)(2,1)S(1)}, bf16[128,840]{1,0:T(8,128)(2,1)}, u32[]{:S(2)}) %copy-start.6) | copy-done | bytes 215064
  42.9 0.0 copy-start.7
  42.9 0.9 %copy-done.7 = f32[210,1]{1,0:T(8,128)S(1)} copy-done((f32[210,1]{1,0:T(8,128)S(1)}, f32[210,1]{1,0:T(8,128)}, u32[]{:S(2)}) %copy-start.7) | copy-done | bytes 864
  43.8 3.5 %update.1 = (f32[1,210,4,840]{3,2,1,0:T(4,128)}, f32[10,21]{1,0:T(8,128)}) custom-call(f32[1,128]{1,0:T(1,128)S(1)} %bitcast.5, f32[210,1]{1,0:T(8,128)S(1)} %copy-done.7, f32[4,210,840]{2,1,0:T(8,128)S(1)} %copy-done, bf16[4,224,128]{2,1,0:T(8,128)(2,1)S(1)} %copy-done.1, bf16[4,224,128]{2,1,0:T(8,128)(2,1)S(1)} %copy-done.2, ...), custom_call_target="tpu_custom_call" | custom-call | tf_op jit(solution)/shard_map/update/pallas_call | solution.py:367
Async XLA Ops:
  0.6 34.7 %copy-start.8 = (f32[128]{0:T(128)S(1)}, f32[128]{0:T(128)}, u32[]{:S(2)}) copy-start(f32[128]{0:T(128)} %param.5) | copy-start | bytes 1540
  35.3 1.9 %copy-start = (f32[4,210,840]{2,1,0:T(8,128)S(1)}, f32[4,210,840]{2,1,0:T(8,128)}, u32[]{:S(2)}) copy-start(f32[4,210,840]{2,1,0:T(8,128)} %get-tuple-element.13.held_ref) | copy-start | bytes 8467204
  37.2 0.9 %copy-start.1 = (bf16[4,224,128]{2,1,0:T(8,128)(2,1)S(1)}, bf16[4,224,128]{2,1,0:T(8,128)(2,1)}, u32[]{:S(2)}) copy-start(bf16[4,224,128]{2,1,0:T(8,128)(2,1)} %get-tuple-element.14.first_col_ref) | copy-start | bytes 688132
  38.2 0.9 %copy-start.2 = (bf16[4,224,128]{2,1,0:T(8,128)(2,1)S(1)}, bf16[4,224,128]{2,1,0:T(8,128)(2,1)}, u32[]{:S(2)}) copy-start(bf16[4,224,128]{2,1,0:T(8,128)(2,1)} %get-tuple-element.15.first_row_ref) | copy-start | bytes 688132
  39.1 0.9 %copy-start.3 = (bf16[4,224,128]{2,1,0:T(8,128)(2,1)S(1)}, bf16[4,224,128]{2,1,0:T(8,128)(2,1)}, u32[]{:S(2)}) copy-start(bf16[4,224,128]{2,1,0:T(8,128)(2,1)} %get-tuple-element.16.second_col_ref) | copy-start | bytes 688132
  40.0 0.9 %copy-start.4 = (bf16[4,224,128]{2,1,0:T(8,128)(2,1)S(1)}, bf16[4,224,128]{2,1,0:T(8,128)(2,1)}, u32[]{:S(2)}) copy-start(bf16[4,224,128]{2,1,0:T(8,128)(2,1)} %get-tuple-element.17.second_row_ref) | copy-start | bytes 688132
  41.0 0.9 %copy-start.5 = (bf16[4,224,128]{2,1,0:T(8,128)(2,1)S(1)}, bf16[4,224,128]{2,1,0:T(8,128)(2,1)}, u32[]{:S(2)}) copy-start(bf16[4,224,128]{2,1,0:T(8,128)(2,1)} %get-tuple-element.18.onehot_col_ref) | copy-start | bytes 688132
  41.9 0.9 %copy-start.6 = (bf16[128,840]{1,0:T(8,128)(2,1)S(1)}, bf16[128,840]{1,0:T(8,128)(2,1)}, u32[]{:S(2)}) copy-start(bf16[128,840]{1,0:T(8,128)(2,1)} %get-tuple-element.19.onehot_row_ref) | copy-start | bytes 645124
  42.9 0.9 %copy-start.7 = (f32[210,1]{1,0:T(8,128)S(1)}, f32[210,1]{1,0:T(8,128)}, u32[]{:S(2)}) copy-start(f32[210,1]{1,0:T(8,128)} %get-tuple-element.12.field_ref) | copy-start | bytes 2524

commit v3 on v2

--- a/solution.py
+++ b/solution.py
@@ -88,8 +88,8 @@
     held, first_col_ref, first_row_ref, second_col_ref, second_row_ref, onehot_col_ref, onehot_row_ref,
     field_out_ref,
     turned, own_t, send_d, recv_d, send_t, recv_t, first_own, second_own,
-    near_send, near_recv, far_send, far_recv,
-    load_sem, d_send, d_recv, t_send, t_recv, near_s, near_r, far_s, far_r,
+    far_send, far_recv,
+    load_sem, d_send, d_recv, t_send, t_recv, far_s, far_r,
     first_row_s, first_row_r, first_col_s, first_col_r,
     second_row_s, second_row_r, second_col_s, second_col_r,
 ):
@@ -158,7 +158,7 @@
             direct = part
         part = dot(col_hot[k], value)
         tall = part if tall is None else tall + part
-    turned[...] = tall.T
+    turned[0:wide] = tall.T
     for c in range(col_count):
         block = turned[c * width : (c + 1) * width]
         own_t[c, 0:width] = block
@@ -209,38 +209,35 @@
     first_wide = first.astype(F32)
     first_tall = first_wide.T.astype(BF16)
 
-    cross = dot(first_tall, own_hot_t)
-    near_send[...] = cross.astype(near_send.dtype)
+    near_copies = [
+        remote(first_own, first_row_ref.at[col], first_col_s.at[k - 1], first_col_r.at[k - 1], {"col": cols[k]})
+        for k in range(1, col_count)
+    ]
     copies = [
-        remote(near_send, near_recv.at[k - 1], near_s.at[k - 1], near_r.at[k - 1], {"col": cols[k]})
-        for k in range(1, col_count)
-    ]
+        remote(first_own, first_col_ref.at[row], first_row_s.at[k - 1], first_row_r.at[k - 1], {"row": rows[k]})
+        for k in range(1, row_count)
+    ]
+    own = first_own[...]
+    first_row_ref[col] = own
+    first_col_ref[row] = own
     pairs = split((dot(own_hot_t, first_tall) + dot(first, own_hot)) * own_mask)
     change = dot(first, gram[0]) - dot(pairs[0], own_hot_t) - dot(pairs[1], own_hot_t)
     if site_count > 256:
         change += dot(first, gram[1])
     fields = decay * fields - rate * jnp.sum(first_wide, axis=1, keepdims=True)
     base = fields + decay * logits - (2.0 * rate) * change
-    for copy in copies:
+    for copy in near_copies:
         copy.wait()
-    for k in range(col_count - 1):
-        cross += near_recv[k].astype(F32)
+    for c in range(col_count):
+        turned[c * width : (c + 1) * width] = first_row_ref[c, 0:width].astype(F32)
+    cross = dot(turned[0:wide].T.astype(BF16), row_hot_t)
     far_send[...] = cross.astype(far_send.dtype)
-    copies = [
+    far_copies = [
         remote(far_send, far_recv.at[k - 1], far_s.at[k - 1], far_r.at[k - 1], {"row": rows[k]})
         for k in range(1, row_count)
     ]
-    far_copies = copies
-    copies = [
-        remote(first_own, first_row_ref.at[col], first_col_s.at[k - 1], first_col_r.at[k - 1], {"col": cols[k]})
-        for k in range(1, col_count)
-    ]
     for copy in far_copies:
         copy.wait()
-    copies += [
-        remote(first_own, first_col_ref.at[row], first_row_s.at[k - 1], first_row_r.at[k - 1], {"row": rows[k]})
-        for k in range(1, row_count)
-    ]
     for k in range(row_count - 1):
         cross += far_recv[k].astype(F32)
     cross = split(cross)
@@ -256,12 +253,9 @@
         remote(second_own, second_row_ref.at[col], second_col_s.at[k - 1], second_col_r.at[k - 1], {"col": cols[k]})
         for k in range(1, col_count)
     ]
-    for own_ref, by_col, by_row in (
-        (first_own, first_col_ref, first_row_ref), (second_own, second_col_ref, second_row_ref)
-    ):
-        own = own_ref[...]
-        by_col[row] = own
-        by_row[col] = own
+    own = second_own[...]
+    second_col_ref[row] = own
+    second_row_ref[col] = own
     field_out_ref[...] = decay * fields - rate * jnp.sum(second, axis=1, keepdims=True)
     for copy in copies:
         copy.wait()
@@ -290,7 +284,7 @@
     for by_row in (first_row_ref, second_row_ref):
         for c in range(col_count):
             stacked[c * width : (c + 1) * width] = by_row[c, 0:width].astype(F32)
-        rights.append(jnp.concatenate([stacked[...].T.astype(BF16), onehot_row_ref[...]], axis=0))
+        rights.append(jnp.concatenate([stacked[0:wide].T.astype(BF16), onehot_row_ref[...]], axis=0))
     stores = []
     for k in range(row_count):
         value = (decay * decay) * held_ref[k]
@@ -321,7 +315,7 @@
     weights = seq_weights.reshape(1, seq_count)
     turned = couplings.transpose(1, 3, 2, 0)
     vmem = pl.BlockSpec(memory_space=pltpu.VMEM)
-    hbm = pl.BlockSpec(memory_space=pltpu.HBM)
+    hbm = pl.BlockSpec(memory_space=pl.ANY)
     dma = pltpu.SemaphoreType.DMA
     row_more, col_more = row_count - 1, col_count - 1
     square = (seq_count, seq_count)
@@ -341,7 +335,7 @@
         in_specs=[vmem, vmem, vmem, hbm],
         out_specs=[vmem] * 8,
         scratch_shapes=[
-            pltpu.VMEM((wide, seq_count), F32),
+            pltpu.VMEM((wide + 24, seq_count), F32),
             pltpu.VMEM((col_count,) + flat, F32),
             pltpu.VMEM((row_more,) + flat, BF16),
             pltpu.VMEM((row_more,) + flat, BF16),
@@ -350,17 +344,15 @@
             pltpu.VMEM(flat, BF16),
             pltpu.VMEM(flat, BF16),
             pltpu.VMEM(square, CROSS),
-            pltpu.VMEM((col_more,) + square, CROSS),
-            pltpu.VMEM(square, CROSS),
             pltpu.VMEM((row_more,) + square, CROSS),
             dma((row_count,)),
             dma((row_more,)), dma((row_more,)), dma((col_more,)), dma((col_more,)),
-            dma((col_more,)), dma((col_more,)), dma((row_more,)), dma((row_more,)),
+            dma((row_more,)), dma((row_more,)),
             dma((row_more,)), dma((row_more,)), dma((col_more,)), dma((col_more,)),
             dma((row_more,)), dma((row_more,)), dma((col_more,)), dma((col_more,)),
         ],
         compiler_params=pltpu.CompilerParams(
-            collective_id=0, has_side_effects=True, vmem_limit_bytes=58 * 1024 * 1024
+            collective_id=0, has_side_effects=True, vmem_limit_bytes=46 * 1024 * 1024
         ),
         name="exchange",
     )(sequences.T, weights, fields, turned)
@@ -374,7 +366,7 @@
         out_specs=[hbm, vmem],
         scratch_shapes=[
             pltpu.VMEM((row_count, width, wide), F32),
-            pltpu.VMEM((wide, seq_count), F32),
+            pltpu.VMEM((wide + 24, seq_count), F32),
             dma((row_count,)),
         ],
         compiler_params=pltpu.CompilerParams(vmem_limit_bytes=40 * 1024 * 1024),

time: 47.6 us -> 38.6 us (0.81)
  Pallas kernels: 38.2 us -> 33.7 us
  local copies, waits for them, and re-layouts: 8.4 us -> 4.08 us
    pallas_call x1, Pallas kernels: 34.7 us -> 30.2 us  [fused_device(): pl.pallas_call(functools.partial(exchange_kernel, sizes), out_shape=[jax....]
    unnamed x18 -> x8, local copies, waits for them, and re-layouts: 8.4 us -> 4.08 us
where the time goes in v3:
time: 38.6 us; the launch traced here: 38.4 us
  Pallas kernels  33.7 us (87%)
  local copies, waits for them, and re-layouts  4.08 us (11%)
  between operations  0.65 us (2%)
    pallas_call x1, Pallas kernels, fused_device(): pl.pallas_call(functools.partial(exchange_kernel, sizes), out_shape=[jax....  30.2 us
    unnamed x8, local copies, waits for them, and re-layouts  4.08 us
    pallas_call x1, Pallas kernels, fused_device(): pl.pallas_call(functools.partial(update_kernel, sizes), out_shape=[jax.Sh...  3.49 us

profile of v3, /device:TPU:0, one launch (start us, length us, event | category | flops | bytes accessed | tf_op | source)
XLA Modules:
  0.0 38.4 jit_solution(3461494145324597095)
XLA Ops:
  0.6 0.0 copy-start
  0.6 1.8 %copy-done = f32[840,1,4,210]{0,2,3,1:T(4,128)S(1)} copy-done((f32[840,1,4,210]{0,2,3,1:T(4,128)S(1)}, f32[840,1,4,210]{0,2,3,1:T(4,128)}, u32[]{:S(2)}) %copy-start) | copy-done | bytes 2822424
  2.5 0.0 copy-start.1
  2.5 0.9 %copy-done.1 = s32[128,160]{0,1:T(8,128)S(1)} copy-done((s32[128,160]{0,1:T(8,128)S(1)}, s32[128,160]{0,1:T(8,128)}, u32[]{:S(2)}) %copy-start.1) | copy-done | bytes 81944
  3.4 0.0 copy-start.2
  3.4 0.7 %copy-done.2 = f32[10,21]{1,0:T(8,128)S(1)} copy-done((f32[10,21]{1,0:T(8,128)S(1)}, f32[10,21]{1,0:T(8,128)}, u32[]{:S(2)}) %copy-start.2) | copy-done | bytes 864
  4.1 0.0 copy-start.3
  4.1 0.7 %copy-done.3 = f32[128]{0:T(128)S(1)} copy-done((f32[128]{0:T(128)S(1)}, f32[128]{0:T(128)}, u32[]{:S(2)}) %copy-start.3) | copy-done | bytes 536
  4.7 30.2 %exchange.1 = (f32[4,210,840]{2,1,0:T(8,128)S(1)}, bf16[4,224,128]{2,1,0:T(8,128)(2,1)S(1)}, bf16[4,224,128]{2,1,0:T(8,128)(2,1)S(1)}, bf16[4,224,128]{2,1,0:T(8...) custom-call(s32[160,128]{1,0:T(8,128)S(1)} %bitcast.5, ...), custom_call_target="tpu_custom_call" | custom-call | tf_op jit(solution)/shard_map/exchange/pallas_call | solution.py:323
  34.9 3.5 %update.1 = (f32[1,210,4,840]{3,2,1,0:T(4,128)}, f32[10,21]{1,0:T(8,128)}) custom-call(f32[1,128]{1,0:T(1,128)S(1)} %bitcast.7, f32[210,1]{1,0:T(8,128)S(1)} %get-tuple-element.12.field_ref, f32[4,210,840]{2,1,0:T(8,128)S(1)} %get-tuple-element.13.held_ref, bf16[4,224,128]{2,1,0:T(8,128)(2,1)S(1)} %get-tuple-element.14.first_col_ref, ...), custom_call_target="tpu_custom_call" | custom-call | tf_op jit(solution)/shard_map/update/pallas_call | solution.py:359
Async XLA Ops:
  0.6 1.9 %copy-start = (f32[840,1,4,210]{0,2,3,1:T(4,128)S(1)}, f32[840,1,4,210]{0,2,3,1:T(4,128)}, u32[]{:S(2)}) copy-start(f32[840,1,4,210]{0,2,3,1:T(4,128)} %param.7) | copy-start | bytes 8467204
  2.5 0.9 %copy-start.1 = (s32[128,160]{0,1:T(8,128)S(1)}, s32[128,160]{0,1:T(8,128)}, u32[]{:S(2)}) copy-start(s32[128,160]{0,1:T(8,128)} %param.4) | copy-start | bytes 245764
  3.4 0.7 %copy-start.2 = (f32[10,21]{1,0:T(8,128)S(1)}, f32[10,21]{1,0:T(8,128)}, u32[]{:S(2)}) copy-start(f32[10,21]{1,0:T(8,128)} %field_ref.1) | copy-start | bytes 2524
  4.1 0.7 %copy-start.3 = (f32[128]{0:T(128)S(1)}, f32[128]{0:T(128)}, u32[]{:S(2)}) copy-start(f32[128]{0:T(128)} %param.5) | copy-start | bytes 1540
